TPU v7x, 32 devices: a whole 2x2x4 slice. The times are simulated.
32 devices in a mesh: grp: 2 (over x), sa: 16 (over z, y, core).
Axes of the slice: x: 2, y: 2, z: 4, core: 2. Of those that a mesh axis runs over, the one named last changes fastest.
Arguments:
- tokens: float32 [16384, 768], P(('grp', 'sa')), parts along dimension 0, may hold values from -6 to 6
- kernel_re: float32 [16384, 768], P(('grp', 'sa')), parts along dimension 0, may hold values from -6 to 6
- kernel_im: float32 [16384, 768], P(('grp', 'sa')), parts along dimension 0, may hold values from -6 to 6
- mix_gain: float32 [768], replicated, may hold values from 0.1 to 1.9
- mlp_gain: float32 [768], replicated, may hold values from 0.1 to 1.9
- w_in: bfloat16 [768, 3072], P('sa'), may hold values from -0.21875 to 0.21875
- w_out: bfloat16 [3072, 768], P('sa'), may hold values from -0.109375 to 0.109375
Outputs:
- layer_out: float32 [16384, 768], P(('grp', 'sa')), parts along dimension 0
There are 2 independent parts, one for each index of `grp`. A program takes and returns all parts, laid end to end along the dimension named above; an argument that names none is the same for every part. Nothing has to cross between parts.
All inputs are finite; a program needn't handle non-finite values.
Results may differ from a plain program's by a relative error of at most 0.0022.
Values may be sent and summed in bfloat16 or wider, within the bound.
A program may use at most 128 MiB of HBM per device.

v0:
```python
import jax
import jax.numpy as jnp
from jax import lax
from jax.sharding import PartitionSpec as P

FACTOR = 32


two_pi = 6.283185307179586
epsilon = 1e-06
highest = lax.Precision.HIGHEST


def rms_scale(values):
    return values * lax.rsqrt(jnp.mean(values * values, axis=-1, keepdims=True) + epsilon)


def phase_pair(first_index, second_index, period):
    phase = (first_index * second_index % period).astype(jnp.float32) * (two_pi / period)
    return (jnp.cos(phase), jnp.sin(phase))


def square_table(length):
    outer_index = lax.broadcasted_iota(jnp.int32, (length, length), 0)
    inner_index = lax.broadcasted_iota(jnp.int32, (length, length), 1)
    return phase_pair(outer_index, inner_index, length)


def contract(pattern, table, values):
    return jnp.einsum(pattern, table, values, precision=highest, preferred_element_type=jnp.float32)


def rotate_sum(pattern, tables, real_part, imag_part, inverse):
    cosine, sine = tables
    cos_real = contract(pattern, cosine, real_part)
    cos_imag = contract(pattern, cosine, imag_part)
    sin_real = contract(pattern, sine, real_part)
    sin_imag = contract(pattern, sine, imag_part)
    if inverse:
        return (cos_real - sin_imag, cos_imag + sin_real)
    return (cos_real + sin_imag, cos_imag - sin_real)


def rotate_each(tables, real_part, imag_part, inverse):
    cosine, sine = tables
    if inverse:
        return (cosine * real_part - sine * imag_part, cosine * imag_part + sine * real_part)
    return (cosine * real_part + sine * imag_part, cosine * imag_part - sine * real_part)


def inner_tables(groups, length):
    outer_index = lax.broadcasted_iota(jnp.int32, (groups, FACTOR, 1), 0)
    inner_index = lax.broadcasted_iota(jnp.int32, (groups, FACTOR, 1), 1)
    return phase_pair(outer_index, inner_index, length)


def local_forward(real_part, imag_part):
    length, channels = real_part.shape
    groups = length // FACTOR
    real_view = real_part.reshape(groups, FACTOR, channels)
    imag_view = imag_part.reshape(groups, FACTOR, channels)
    real_mid, imag_mid = rotate_sum(
        "ca,abd->cbd", square_table(groups), real_view, imag_view, False
    )
    real_mid, imag_mid = rotate_each(inner_tables(groups, length), real_mid, imag_mid, False)
    real_out, imag_out = rotate_sum("eb,cbd->ecd", square_table(FACTOR), real_mid, imag_mid, False)
    return (real_out.reshape(length, channels), imag_out.reshape(length, channels))


def local_inverse(real_part, imag_part):
    length, channels = real_part.shape
    groups = length // FACTOR
    real_view = real_part.reshape(FACTOR, groups, channels)
    imag_view = imag_part.reshape(FACTOR, groups, channels)
    real_mid, imag_mid = rotate_sum("be,ecd->cbd", square_table(FACTOR), real_view, imag_view, True)
    real_mid, imag_mid = rotate_each(inner_tables(groups, length), real_mid, imag_mid, True)
    real_out, imag_out = rotate_sum("ac,cbd->abd", square_table(groups), real_mid, imag_mid, True)
    return (real_out.reshape(length, channels), imag_out.reshape(length, channels))


def on_device(tokens, kernel_re, kernel_im, mix_gain, mlp_gain, w_in, w_out):
    shards = lax.axis_size("sa")
    position = lax.axis_index("sa")
    local_rows, channels = tokens.shape
    stride = local_rows // shards
    seq_total = shards * local_rows
    normed = rms_scale(tokens) * mix_gain
    received = lax.all_to_all(
        normed.reshape(1, shards, stride, channels), "sa", split_axis=1, concat_axis=0, tiled=True
    )
    cosine, sine = square_table(shards)
    real_part = contract("kp,pard->kard", cosine, received)
    imag_part = -contract("kp,pard->kard", sine, received)
    freq_index = lax.broadcasted_iota(jnp.int32, (shards, 1, stride, 1), 0)
    row_index = lax.broadcasted_iota(jnp.int32, (shards, 1, stride, 1), 2) + position * stride
    spread_real, spread_imag = rotate_each(
        phase_pair(freq_index, row_index, seq_total), real_part, imag_part, False
    )
    real_part = lax.all_to_all(spread_real, "sa", split_axis=0, concat_axis=1, tiled=True)
    imag_part = lax.all_to_all(spread_imag, "sa", split_axis=0, concat_axis=1, tiled=True)
    coeff_real, coeff_imag = local_forward(
        real_part.reshape(local_rows, -1), imag_part.reshape(local_rows, -1)
    )
    moved_real, moved_imag = (
        lax.all_to_all(
            kernel_re.reshape(1, stride, shards, channels),
            "sa",
            split_axis=2,
            concat_axis=0,
            tiled=True,
        ),
        lax.all_to_all(
            kernel_im.reshape(1, stride, shards, channels),
            "sa",
            split_axis=2,
            concat_axis=0,
            tiled=True,
        ),
    )
    moved_real = moved_real.reshape(local_rows, channels)
    moved_imag = moved_imag.reshape(local_rows, channels)
    filtered_real = coeff_real * moved_real - coeff_imag * moved_imag
    filtered_imag = coeff_real * moved_imag + coeff_imag * moved_real
    inverse_real, inverse_imag = local_inverse(filtered_real, filtered_imag)
    row_index = lax.broadcasted_iota(jnp.int32, (local_rows, 1), 0)
    inverse_real, inverse_imag = rotate_each(
        phase_pair(row_index, position, seq_total), inverse_real, inverse_imag, True
    )
    real_part = lax.all_to_all(
        inverse_real.reshape(1, shards, stride, channels),
        "sa",
        split_axis=1,
        concat_axis=0,
        tiled=True,
    )
    imag_part = lax.all_to_all(
        inverse_imag.reshape(1, shards, stride, channels),
        "sa",
        split_axis=1,
        concat_axis=0,
        tiled=True,
    )
    cosine, sine = square_table(shards)
    summed = contract("pk,kard->pard", cosine, real_part) - contract(
        "pk,kard->pard", sine, imag_part
    )
    conv_spread = summed / seq_total
    conv = lax.all_to_all(conv_spread, "sa", split_axis=0, concat_axis=1, tiled=True).reshape(
        local_rows, channels
    )
    mixed = tokens + conv * jax.nn.sigmoid(normed)
    scaled = (rms_scale(mixed) * mlp_gain).astype(jnp.bfloat16)
    columns = scaled
    hidden_pre = jnp.dot(
        columns, lax.all_gather(w_in, "sa", axis=0, tiled=True), preferred_element_type=jnp.float32
    )
    hidden = jax.nn.gelu(hidden_pre, approximate=True).astype(jnp.bfloat16)
    columns = hidden
    branch_out = jnp.dot(
        columns, lax.all_gather(w_out, "sa", axis=0, tiled=True), preferred_element_type=jnp.float32
    )
    return mixed + branch_out


def solution(mesh):
    return jax.shard_map(
        on_device,
        mesh=mesh,
        in_specs=(
            P(("grp", "sa"), None),
            P(("grp", "sa"), None),
            P(("grp", "sa"), None),
            P(),
            P(),
            P("sa", None),
            P("sa", None),
        ),
        out_specs=P(("grp", "sa"), None),
        check_vma=False,
    )
```

profile of v0, /device:TPU:1, one launch (start us, length us, event | category | flops | bytes accessed | tf_op | source)
XLA Modules:
  0.0 434.4 jit_solution(15403068367278759685)
XLA Ops:
  9.8 7.3 %all-to-all-start = ((f32[1,16,32,768]{3,2,0,1:T(8,128)}), f32[1,16,32,768]{3,2,0,1:T(8,128)S(1)}, u32[]{:S(2)}, u32[]{:S(2)}) async-start(f32[1,16,32,768]{3,2,0,1:T(8,128)} %bitcast.127), calls=%async_computation | async-start | bytes 3145728 | tf_op jit(solution)/shard_map/all_to_all | solution.py:88
  20.6 28.8 %all-to-all-done = f32[1,16,32,768]{3,2,0,1:T(8,128)S(1)} async-done(((f32[1,16,32,768]{3,2,0,1:T(8,128)}), f32[1,16,32,768]{3,2,0,1:T(8,128)S(1)}, u32[]{:S(2)}, u32[]{:S(2)}) %all-to-all-start) | async-done | bytes 1572896 | tf_op jit(solution)/shard_map/all_to_all | solution.py:88
  49.4 8.8 %all-to-all-start.3 = ((f32[1,32,16,768]{3,1,0,2:T(8,128)}), f32[1,32,16,768]{3,1,0,2:T(8,128)}, u32[]{:S(2)}, u32[]{:S(2)}) async-start(f32[1,32,16,768]{3,1,0,2:T(8,128)} %copy.92), calls=%async_computation.3 | async-start | bytes 3145728 | tf_op jit(solution)/shard_map/all_to_all | solution.py:105
  60.6 3.7 add_bitcast_fusion.2
  66.4 24.3 %all-to-all-done.3 = f32[1,32,16,768]{3,1,0,2:T(8,128)} async-done(((f32[1,32,16,768]{3,1,0,2:T(8,128)}), f32[1,32,16,768]{3,1,0,2:T(8,128)}, u32[]{:S(2)}, u32[]{:S(2)}) %all-to-all-start.3) | async-done | bytes 1572896 | tf_op jit(solution)/shard_map/all_to_all | solution.py:105
  90.6 8.8 %all-to-all-start.2 = ((f32[16,1,32,768]{3,2,1,0:T(8,128)}), f32[16,1,32,768]{3,2,1,0:T(8,128)S(1)}, u32[]{:S(2)}, u32[]{:S(2)}) async-start(f32[16,1,32,768]{3,2,1,0:T(8,128)} %copy.87), calls=%async_computation.2 | async-start | bytes 3145728 | tf_op jit(solution)/shard_map/all_to_all | solution.py:100
  99.4 3.6 copy.85
  103.0 28.8 %all-to-all-done.2 = f32[16,1,32,768]{3,2,1,0:T(8,128)S(1)} async-done(((f32[16,1,32,768]{3,2,1,0:T(8,128)}), f32[16,1,32,768]{3,2,1,0:T(8,128)S(1)}, u32[]{:S(2)}, u32[]{:S(2)}) %all-to-all-start.2) | async-done | bytes 1572896 | tf_op jit(solution)/shard_map/all_to_all | solution.py:100
  131.7 8.8 %all-to-all-start.1 = ((f32[16,1,32,768]{3,2,1,0:T(8,128)}), f32[16,1,32,768]{3,2,1,0:T(8,128)}, u32[]{:S(2)}, u32[]{:S(2)}) async-start(f32[16,1,32,768]{3,2,1,0:T(8,128)} %copy.85), calls=%async_computation.1 | async-start | bytes 3145728 | tf_op jit(solution)/shard_map/all_to_all | solution.py:99
  144.7 37.7 %all-to-all-done.1 = f32[16,1,32,768]{3,2,1,0:T(8,128)} async-done(((f32[16,1,32,768]{3,2,1,0:T(8,128)}), f32[16,1,32,768]{3,2,1,0:T(8,128)}, u32[]{:S(2)}, u32[]{:S(2)}) %all-to-all-start.1) | async-done | bytes 1572896 | tf_op jit(solution)/shard_map/all_to_all | solution.py:99
  182.4 8.9 %all-to-all-start.4 = ((f32[1,32,16,768]{3,1,0,2:T(8,128)}), f32[1,32,16,768]{3,1,0,2:T(8,128)}, u32[]{:S(2)}, u32[]{:S(2)}) async-start(f32[1,32,16,768]{3,1,0,2:T(8,128)} %copy.96), calls=%async_computation.4 | async-start | bytes 3145728 | tf_op jit(solution)/shard_map/all_to_all | solution.py:112
  196.2 3.6 fusion.29
  199.8 3.9 multiply_add_fusion.1
  206.1 3.9 fusion.46
  213.4 21.7 %all-to-all-done.4 = f32[1,32,16,768]{3,1,0,2:T(8,128)} async-done(((f32[1,32,16,768]{3,1,0,2:T(8,128)}), f32[1,32,16,768]{3,1,0,2:T(8,128)}, u32[]{:S(2)}, u32[]{:S(2)}) %all-to-all-start.4) | async-done | bytes 1572896 | tf_op jit(solution)/shard_map/all_to_all | solution.py:112
  235.1 6.9 %multiply_subtract_fusion = (f32[32,16,768]{2,0,1:T(8,128)S(1)}, f32[32,16,768]{2,0,1:T(8,128)S(1)}) fusion(f32[32,16,768]{2,0,1:T(8,128)} %convolution_add_fusion.2, f32[32,16,768]{2,1,0:T(8,128)} %bitcast.18, f32[32,16,768]{2,1,0:T(8,128)} %bitcast.14, f32[32,16,768]{2,0,1:T(8,128)} %fusion.46, f32[16,32,768]{2,0,1:T(8,128)S(1)} %get-tuple-element.11), kind=kOutput, calls=%fused_computation.38 | convolution fusion | flops 153761792 | bytes 11010048 | tf_op jit(solution)/shard_map/eb,cbd->ecd/dot_general | solution.py:30
  255.7 3.9 subtract_bitcast_fusion
  261.7 9.1 %all-to-all-start.6 = ((f32[1,16,32,768]{3,2,0,1:T(8,128)}), f32[1,16,32,768]{3,2,0,1:T(8,128)S(1)}, u32[]{:S(2)}, u32[]{:S(2)}) async-start(f32[1,16,32,768]{3,2,0,1:T(8,128)} %copy.107), calls=%async_computation.6 | async-start | bytes 3145728 | tf_op jit(solution)/shard_map/all_to_all | solution.py:136
  275.0 37.6 %all-to-all-done.6 = f32[1,16,32,768]{3,2,0,1:T(8,128)S(1)} async-done(((f32[1,16,32,768]{3,2,0,1:T(8,128)}), f32[1,16,32,768]{3,2,0,1:T(8,128)S(1)}, u32[]{:S(2)}, u32[]{:S(2)}) %all-to-all-start.6) | async-done | bytes 1572896 | tf_op jit(solution)/shard_map/all_to_all | solution.py:136
  312.6 8.8 %all-to-all-start.5 = ((f32[1,16,32,768]{3,2,0,1:T(8,128)}), f32[1,16,32,768]{3,2,0,1:T(8,128)}, u32[]{:S(2)}, u32[]{:S(2)}) async-start(f32[1,16,32,768]{3,2,0,1:T(8,128)} %copy.105), calls=%async_computation.5 | async-start | bytes 3145728 | tf_op jit(solution)/shard_map/all_to_all | solution.py:129
  324.7 40.7 %all-to-all-done.5 = f32[1,16,32,768]{3,2,0,1:T(8,128)} async-done(((f32[1,16,32,768]{3,2,0,1:T(8,128)}), f32[1,16,32,768]{3,2,0,1:T(8,128)}, u32[]{:S(2)}, u32[]{:S(2)}) %all-to-all-start.5) | async-done | bytes 1572896 | tf_op jit(solution)/shard_map/all_to_all | solution.py:129
  365.4 4.1 multiply_bitcast_fusion
  370.4 45.6 %all_to_all.84 = f32[16,1,32,768]{3,2,1,0:T(8,128)S(1)} all-to-all(f32[16,1,32,768]{3,2,1,0:T(8,128)S(1)} %copy.109), channel_id=1, replica_groups=mesh['grp'=2,'sa'=16] {'sa'}, dimensions={0} | all-to-all | bytes 3145728 | tf_op jit(solution)/shard_map/all_to_all | solution.py:148
  416.8 10.2 %fusion.58 = f32[512,768]{1,0:T(8,128)} fusion(f32[512,768]{1,0:T(8,128)S(1)} %get-tuple-element.6, bf16[3072,768]{1,0:T(8,128)(2,1)} %all-gather.5.cloned.1.call-done, bf16[768,3072]{1,0:T(8,128)(2,1)} %all-gather.3.cloned.1.call-done, f32[768]{0:T(1024)S(1)} %copy-done.2, f32[512]{0:T(512)S(1)} %add_rsqrt_fusion), kind=kOutput, calls=%fused_computation.72 | convolution fusion | flops 4847566848 | bytes 12588032 | tf_op jit(solution)/shard_map/dot_general | solution.py:159
  (46 shorter events, 50.9 us)
Async XLA Ops:
  6.5 1.9 copy-start
  6.5 1.9 copy-start.1
  9.8 39.7 %all-to-all-start = ((f32[1,16,32,768]{3,2,0,1:T(8,128)}), f32[1,16,32,768]{3,2,0,1:T(8,128)S(1)}, u32[]{:S(2)}, u32[]{:S(2)}) async-start(f32[1,16,32,768]{3,2,0,1:T(8,128)} %bitcast.127), calls=%async_computation | async-start | bytes 3145728 | tf_op jit(solution)/shard_map/all_to_all | solution.py:88
  49.4 41.2 %all-to-all-start.3 = ((f32[1,32,16,768]{3,1,0,2:T(8,128)}), f32[1,32,16,768]{3,1,0,2:T(8,128)}, u32[]{:S(2)}, u32[]{:S(2)}) async-start(f32[1,32,16,768]{3,1,0,2:T(8,128)} %copy.92), calls=%async_computation.3 | async-start | bytes 3145728 | tf_op jit(solution)/shard_map/all_to_all | solution.py:105
  90.6 41.1 %all-to-all-start.2 = ((f32[16,1,32,768]{3,2,1,0:T(8,128)}), f32[16,1,32,768]{3,2,1,0:T(8,128)S(1)}, u32[]{:S(2)}, u32[]{:S(2)}) async-start(f32[16,1,32,768]{3,2,1,0:T(8,128)} %copy.87), calls=%async_computation.2 | async-start | bytes 3145728 | tf_op jit(solution)/shard_map/all_to_all | solution.py:100
  131.7 50.7 %all-to-all-start.1 = ((f32[16,1,32,768]{3,2,1,0:T(8,128)}), f32[16,1,32,768]{3,2,1,0:T(8,128)}, u32[]{:S(2)}, u32[]{:S(2)}) async-start(f32[16,1,32,768]{3,2,1,0:T(8,128)} %copy.85), calls=%async_computation.1 | async-start | bytes 3145728 | tf_op jit(solution)/shard_map/all_to_all | solution.py:99
  140.5 276.3 %all-gather.3.cloned.1.call-start = ((), (), s32[]{:S(2)}) async-start(), calls=%async_computation.8 | async-start | bytes 5013504 | tf_op jit(solution)/shard_map/all_gather | solution.py:155
  182.4 52.7 %all-to-all-start.4 = ((f32[1,32,16,768]{3,1,0,2:T(8,128)}), f32[1,32,16,768]{3,1,0,2:T(8,128)}, u32[]{:S(2)}, u32[]{:S(2)}) async-start(f32[1,32,16,768]{3,1,0,2:T(8,128)} %copy.96), calls=%async_computation.4 | async-start | bytes 3145728 | tf_op jit(solution)/shard_map/all_to_all | solution.py:112
  261.7 50.9 %all-to-all-start.6 = ((f32[1,16,32,768]{3,2,0,1:T(8,128)}), f32[1,16,32,768]{3,2,0,1:T(8,128)S(1)}, u32[]{:S(2)}, u32[]{:S(2)}) async-start(f32[1,16,32,768]{3,2,0,1:T(8,128)} %copy.107), calls=%async_computation.6 | async-start | bytes 3145728 | tf_op jit(solution)/shard_map/all_to_all | solution.py:136
  270.8 146.0 %all-gather.5.cloned.1.call-start = ((), (), s32[]{:S(2)}) async-start(), calls=%async_computation.9 | async-start | bytes 5013504 | tf_op jit(solution)/shard_map/all_gather | solution.py:160
  312.6 52.8 %all-to-all-start.5 = ((f32[1,16,32,768]{3,2,0,1:T(8,128)}), f32[1,16,32,768]{3,2,0,1:T(8,128)}, u32[]{:S(2)}, u32[]{:S(2)}) async-start(f32[1,16,32,768]{3,2,0,1:T(8,128)} %copy.105), calls=%async_computation.5 | async-start | bytes 3145728 | tf_op jit(solution)/shard_map/all_to_all | solution.py:129
  416.0 0.8 copy-start.2
Sparse Core Ops, SparseCore 0:
  143.6 87.5 all-gather.2
  273.9 87.8 all-gather.4
where the time goes:
time: 443 us; the launch traced here: 434 us
  waiting for transfers between devices  221 us (50%)
  matrix products  69.5 us (16%)
  starting transfers between devices  60.6 us (14%)
  blocking collectives  45.6 us (10%)
  local copies, waits for them, and re-layouts  19.7 us (4%)
  between operations  14 us (3%)
    dot_general x20, matrix products, contract(): jnp.einsum(pattern, table, values, precision=highest, preferred_element_t...  59.2 us
    all_to_all x1, blocking collectives, on_device(): lax.all_to_all(conv_spread, 'sa', split_axis=0, concat_axis=1, tiled=True)  45.6 us
    all_to_all x1, waiting for transfers between devices, on_device(): lax.all_to_all(inverse_real.reshape(1, shards, stride, channels), 'sa', s...  40.7 us
    all_to_all x1, waiting for transfers between devices, on_device(): lax.all_to_all(spread_real, 'sa', split_axis=0, concat_axis=1, tiled=True)  37.7 us
    all_to_all x1, waiting for transfers between devices, on_device(): lax.all_to_all(inverse_imag.reshape(1, shards, stride, channels), 'sa', s...  37.6 us
    all_to_all x1, waiting for transfers between devices, on_device(): lax.all_to_all(normed.reshape(1, shards, stride, channels), 'sa', split_a...  28.8 us
    all_to_all x1, waiting for transfers between devices, on_device(): lax.all_to_all(spread_imag, 'sa', split_axis=0, concat_axis=1, tiled=True)  28.8 us
    all_to_all x1, waiting for transfers between devices, on_device(): lax.all_to_all(kernel_re.reshape(1, stride, shards, channels), 'sa', spli...  24.3 us
  transfers between devices with their start and end apart: 9, of which 7 were waited for; matrix products, arithmetic and copies ran while one was open for 18% of the time, Pallas kernels for 0%

commit v1 on v0

v1 whole, which is shorter than its diff:
```python
import jax
import jax.numpy as jnp
import numpy as np
from jax import lax
from jax.sharding import PartitionSpec as P

LANES = 128
EPSILON = 1e-06
LINK = jnp.float16
CONV_SCALE = 0.125


def rms_scale(values):
    return values * lax.rsqrt(jnp.mean(values * values, axis=-1, keepdims=True) + EPSILON)


def angles(first, second, period):
    product = np.outer(np.arange(first, dtype=np.int64), np.arange(second, dtype=np.int64)) % period
    phase = product.astype(np.float64) * (2 * np.pi / period)
    return np.cos(phase), np.sin(phase)


def contract(pattern, left, right):
    return jnp.einsum(
        pattern, left, right, precision=lax.Precision.HIGH, preferred_element_type=jnp.float32
    )


def on_device(tokens, kernel_re, kernel_im, mix_gain, mlp_gain, w_in, w_out):
    shards = lax.axis_size("sa")
    rows, channels = tokens.shape
    part = channels // shards
    blocks = rows // LANES
    total = shards * rows
    outer = total // LANES

    def to_channels(values):
        packed = values.astype(LINK).reshape(blocks, LANES, shards, part).transpose(2, 0, 3, 1)
        moved = lax.all_to_all(packed, "sa", split_axis=0, concat_axis=0, tiled=True)
        return moved.reshape(outer, part, LANES)

    normed = rms_scale(tokens) * mix_gain
    signal = to_channels(normed).astype(jnp.float32)

    def by_frequency(moved):
        ordered = moved.transpose(1, 0, 2).reshape(part, LANES, outer)
        return ordered.transpose(2, 0, 1).astype(jnp.float32)

    filter_re = by_frequency(to_channels(kernel_re))
    filter_im = by_frequency(to_channels(kernel_im))

    cos_outer, sin_outer = angles(outer, outer, outer)
    cos_inner, sin_inner = angles(LANES, LANES, LANES)
    cos_twist, sin_twist = angles(outer, LANES, total)
    first = jnp.asarray(np.concatenate([cos_outer, -sin_outer], 0), jnp.float32)
    last = jnp.asarray(np.concatenate([cos_outer, -sin_outer], 1), jnp.float32)
    forward = jnp.asarray(
        np.block([[cos_inner, -sin_inner], [sin_inner, cos_inner]]), jnp.float32
    )
    backward = jnp.asarray(
        np.block([[cos_inner, sin_inner], [-sin_inner, cos_inner]]), jnp.float32
    )
    cos_twist = jnp.asarray(cos_twist[:, None, :], jnp.float32)
    sin_twist = jnp.asarray(sin_twist[:, None, :], jnp.float32)

    mid = contract("ca,adb->cdb", first, signal)
    mid_re, mid_im = mid[:outer], mid[outer:]
    turned = jnp.concatenate(
        [mid_re * cos_twist + mid_im * sin_twist, mid_im * cos_twist - mid_re * sin_twist], -1
    )
    spectrum = contract("cdb,be->cde", turned, forward)
    spec_re, spec_im = spectrum[..., :LANES], spectrum[..., LANES:]
    filtered = jnp.concatenate(
        [spec_re * filter_re - spec_im * filter_im, spec_re * filter_im + spec_im * filter_re], -1
    )
    back = contract("cde,eb->cdb", filtered, backward)
    back_re, back_im = back[..., :LANES], back[..., LANES:]
    untwisted = jnp.concatenate(
        [back_re * cos_twist - back_im * sin_twist, back_im * cos_twist + back_re * sin_twist], 0
    )
    conv = contract("ac,cdb->adb", last, untwisted)
    conv = (conv * (CONV_SCALE / total)).astype(LINK).reshape(shards, blocks, part, LANES)
    conv = lax.all_to_all(conv, "sa", split_axis=0, concat_axis=0, tiled=True)
    conv = conv.transpose(1, 3, 0, 2).reshape(rows, channels).astype(jnp.float32) * (1 / CONV_SCALE)

    mixed = tokens + conv * jax.nn.sigmoid(normed)
    scaled = (rms_scale(mixed) * mlp_gain).astype(jnp.bfloat16)
    hidden_pre = jnp.dot(
        scaled, lax.all_gather(w_in, "sa", axis=0, tiled=True), preferred_element_type=jnp.float32
    )
    hidden = jax.nn.gelu(hidden_pre, approximate=True).astype(jnp.bfloat16)
    branch = jnp.dot(
        hidden, lax.all_gather(w_out, "sa", axis=0, tiled=True), preferred_element_type=jnp.float32
    )
    return mixed + branch


def solution(mesh):
    return jax.shard_map(
        on_device,
        mesh=mesh,
        in_specs=(
            P(("grp", "sa"), None),
            P(("grp", "sa"), None),
            P(("grp", "sa"), None),
            P(),
            P(),
            P("sa", None),
            P("sa", None),
        ),
        out_specs=P(("grp", "sa"), None),
        check_vma=False,
    )
```

time: 443 us -> 190 us (0.43); the launches traced: 434 us -> 189 us
  waiting for transfers between devices: 221 us -> 61.2 us
  matrix products: 69.5 us -> 18.8 us
  starting transfers between devices: 60.6 us -> 23.3 us
  blocking collectives: 45.6 us -> 36 us
  other arithmetic: 3.97 us -> 10.3 us
  local copies, waits for them, and re-layouts: 19.7 us -> 25.6 us
    all_to_all x7 -> x3, waiting for transfers between devices: 220 us -> 59.8 us  [to_channels(): lax.all_to_all(packed, 'sa', split_axis=0, concat_axis=0, tiled=True)]
    dot_general x21 -> x5, matrix products: 69.5 us -> 18.8 us  [the longest x1 10.3 us: on_device(): jnp.dot(hidden, lax.all_gather(w_out, 'sa', axis=0, tiled=True), preferre...]
    all_to_all x7 -> x3, starting transfers between devices: 60.5 us -> 23.2 us  [to_channels(): lax.all_to_all(packed, 'sa', split_axis=0, concat_axis=0, tiled=True)]
    convert_element_type x0 -> x9, local copies, waits for them, and re-layouts: none -> 16.3 us  [the longest x6 13.1 us: by_frequency(): return ordered.transpose(2, 0, 1).astype(jnp.float32)]
    all_to_all x1, blocking collectives: 45.6 us -> 36 us  [on_device(): conv = lax.all_to_all(conv, 'sa', split_axis=0, concat_axis=0, tiled=True)]
    add x2 -> x0, local copies, waits for them, and re-layouts: 5.65 us -> none  [the longest x1 3.58 us: rotate_each(): cosine * real_part + sine * imag_part]
    convert_element_type x0 -> x5, other arithmetic: none -> 5.59 us  [the longest x3 4.19 us: to_channels(): values.astype(LINK).reshape(blocks, LANES, shards, part)]
    sub x2 -> x0, local copies, waits for them, and re-layouts: 5.56 us -> none  [the longest x1 3.49 us: rotate_each(): cosine * real_part - sine * imag_part]
  transfers between devices with their start and end apart: 9 -> 5, of which waited for: 7 -> 3; matrix products, arithmetic and copies ran while one was open for 18% -> 23% of each run, Pallas kernels for 0% -> 0%
where the time goes in v1:
time: 190 us; the launch traced here: 189 us
  waiting for transfers between devices  61.2 us (32%)
  blocking collectives  36 us (19%)
  local copies, waits for them, and re-layouts  25.6 us (13%)
  starting transfers between devices  23.3 us (12%)
  matrix products  18.8 us (10%)
  between operations  13.7 us (7%)
  other arithmetic  10.3 us (5%)
    all_to_all x3, waiting for transfers between devices, to_channels(): lax.all_to_all(packed, 'sa', split_axis=0, concat_axis=0, tiled=True)  59.8 us
    all_to_all x1, blocking collectives, on_device(): conv = lax.all_to_all(conv, 'sa', split_axis=0, concat_axis=0, tiled=True)  36 us
    all_to_all x3, starting transfers between devices, to_channels(): lax.all_to_all(packed, 'sa', split_axis=0, concat_axis=0, tiled=True)  23.2 us
    convert_element_type x6, local copies, waits for them, and re-layouts, by_frequency(): return ordered.transpose(2, 0, 1).astype(jnp.float32)  13.1 us
    dot_general x1, matrix products, on_device(): jnp.dot(hidden, lax.all_gather(w_out, 'sa', axis=0, tiled=True), preferre...  10.3 us
    dot_general x4, matrix products, contract(): jnp.einsum(pattern, left, right, precision=lax.Precision.HIGH, preferred_...  8.5 us
    convert_element_type x3, other arithmetic, to_channels(): values.astype(LINK).reshape(blocks, LANES, shards, part)  4.19 us
    reshape x5, local copies, waits for them, and re-layouts, to_channels(): values.astype(LINK).reshape(blocks, LANES, shards, part)  3.91 us
  transfers between devices with their start and end apart: 5, of which 3 were waited for; matrix products, arithmetic and copies ran while one was open for 23% of the time, Pallas kernels for 0%

profile of v1, /device:TPU:1, one launch (start us, length us, event | category | flops | bytes accessed | tf_op | source)
XLA Modules:
  0.0 188.8 jit_solution(3008938105487784878)
XLA Ops:
  7.3 1.5 convert_element_type.58
  10.8 7.3 %all-to-all-start.1 = ((f16[16,4,48,128]{3,2,1,0:T(8,128)(2,1)}), f16[16,4,48,128]{3,2,1,0:T(8,128)(2,1)S(1)}, u32[]{:S(2)}, u32[]{:S(2)}) async-start(f16[16,4,48,128]{3,2,1,0:T(8,128)(2,1)} %bitcast.59), calls=%async_computation.1 | async-start | bytes 1572864 | tf_op jit(solution)/shard_map/all_to_all | solution.py:39
  18.9 1.6 convert_element_type.64
  21.4 1.1 copy.60
  22.6 23.6 %all-to-all-done.1 = f16[16,4,48,128]{3,2,1,0:T(8,128)(2,1)S(1)} async-done(((f16[16,4,48,128]{3,2,1,0:T(8,128)(2,1)}), f16[16,4,48,128]{3,2,1,0:T(8,128)(2,1)S(1)}, u32[]{:S(2)}, u32[]{:S(2)}) %all-to-all-start.1) | async-done | bytes 786464 | tf_op jit(solution)/shard_map/all_to_all | solution.py:39
  46.2 5.7 %all-to-all-start.2 = ((f16[16,4,48,128]{3,2,1,0:T(8,128)(2,1)}), f16[16,4,48,128]{3,2,1,0:T(8,128)(2,1)}, u32[]{:S(2)}, u32[]{:S(2)}) async-start(f16[16,4,48,128]{3,2,1,0:T(8,128)(2,1)} %bitcast.58), calls=%async_computation.2 | async-start | bytes 1572864 | tf_op jit(solution)/shard_map/all_to_all | solution.py:39
  53.3 1.8 copy.34
  56.2 26.4 %all-to-all-done.2 = f16[16,4,48,128]{3,2,1,0:T(8,128)(2,1)} async-done(((f16[16,4,48,128]{3,2,1,0:T(8,128)(2,1)}), f16[16,4,48,128]{3,2,1,0:T(8,128)(2,1)}, u32[]{:S(2)}, u32[]{:S(2)}) %all-to-all-start.2) | async-done | bytes 786464 | tf_op jit(solution)/shard_map/all_to_all | solution.py:39
  82.7 10.1 %all-to-all-start = ((f16[16,4,48,128]{3,1,2,0:T(4,128)(2,1)}), f16[16,4,48,128]{3,1,2,0:T(4,128)(2,1)}, u32[]{:S(2)}, u32[]{:S(2)}) async-start(f16[16,4,48,128]{3,1,2,0:T(4,128)(2,1)} %bitcast.1), calls=%async_computation | async-start | bytes 1572864 | tf_op jit(solution)/shard_map/all_to_all | solution.py:39
  93.5 2.0 %reshape.54 = f32[48,128,64]{2,1,0:T(8,128)} reshape(f32[48,64,128]{2,1,0:T(8,128)S(1)} %copy.39) | data formatting | bytes 3145728 | tf_op jit(solution)/shard_map/convert_element_type | solution.py:47
  95.4 2.4 %copy.40 = f32[48,128,64]{1,0,2:T(8,128)S(1)} copy(f32[48,128,64]{2,1,0:T(8,128)} %reshape.54) | data formatting | bytes 3145728 | tf_op jit(solution)/shard_map/convert_element_type | solution.py:47
  97.9 1.2 convert_bitcast_fusion
  99.1 1.6 copy.43
  100.7 3.4 %reshape.55 = f32[48,128,64]{2,1,0:T(8,128)} reshape(f32[48,64,128]{2,1,0:T(8,128)} %copy.43) | data formatting | bytes 3145728 | tf_op jit(solution)/shard_map/convert_element_type | solution.py:47
  104.1 3.2 %copy.44 = f32[48,128,64]{1,0,2:T(8,128)} copy(f32[48,128,64]{2,1,0:T(8,128)} %reshape.55) | data formatting | bytes 3145728 | tf_op jit(solution)/shard_map/convert_element_type | solution.py:47
  107.4 9.7 %all-to-all-done = f16[16,4,48,128]{3,1,2,0:T(4,128)(2,1)} async-done(((f16[16,4,48,128]{3,1,2,0:T(4,128)(2,1)}), f16[16,4,48,128]{3,1,2,0:T(4,128)(2,1)}, u32[]{:S(2)}, u32[]{:S(2)}) %all-to-all-start) | async-done | bytes 786464 | tf_op jit(solution)/shard_map/all_to_all | solution.py:39
  117.1 1.6 copy.35
  118.7 1.5 fusion.36
  121.9 3.0 %fusion.14 = f32[64,48,256]{2,1,0:T(8,128)S(1)} fusion(f32[256,256,1]{1,0,2:T(8,128)S(1)} %copy-done.3, f32[64,48,256]{2,0,1:T(8,128)S(1)} %pad_maximum_fusion), kind=kOutput, calls=%fused_computation.17 | convolution fusion | flops 1207959552 | bytes 6553600 | tf_op jit(solution)/shard_map/cdb,be->cde/dot_general | solution.py:24
  126.2 3.0 %fusion.12 = f32[64,48,256]{2,0,1:T(8,128)S(1)} fusion(f32[256,256,1]{1,0,2:T(8,128)S(1)} %copy-done.2, f32[64,48,256]{2,1,0:T(8,128)S(1)} %pad_maximum_fusion.1), kind=kOutput, calls=%fused_computation.15 | convolution fusion | flops 1207959552 | bytes 6553600 | tf_op jit(solution)/shard_map/cde,eb->cdb/dot_general | solution.py:24
  131.4 36.0 %all_to_all.20 = f16[16,4,48,128]{3,1,2,0:T(4,128)(2,1)S(1)} all-to-all(f16[16,4,48,128]{3,1,2,0:T(4,128)(2,1)S(1)} %copy.47), channel_id=1, replica_groups=mesh['grp'=2,'sa'=16] {'sa'}, dimensions={0} | all-to-all | bytes 1572864 | tf_op jit(solution)/shard_map/all_to_all | solution.py:83
  167.9 1.6 copy.48
  169.5 2.1 %multiply_reduce_fusion = (f32[512]{0:T(512)S(1)}, f32[512,768]{1,0:T(8,128)S(1)}) fusion(f32[512,768]{1,0:T(8,128)S(1)} %copy-done, f32[512,768]{1,0:T(8,128)} %copy.48, f32[768]{0:T(1024)S(1)} %copy-done.8, f32[512]{0:T(512)S(1)} %add_rsqrt_fusion.1), kind=kLoop, calls=%fused_computation.30 | loop fusion | flops 3538432 | bytes 4725760 | tf_op jit(solution)/shard_map/reduce_sum | solution.py:14
  171.7 10.3 %fusion.23 = f32[512,768]{1,0:T(8,128)} fusion(f32[512,768]{1,0:T(8,128)S(1)} %get-tuple-element.6, bf16[3072,768]{1,0:T(8,128)(2,1)} %all-gather.5.cloned.1.call-done, bf16[768,3072]{1,0:T(8,128)(2,1)} %all-gather.3.cloned.1.call-done, f32[768]{0:T(1024)S(1)} %copy-done.9, f32[512]{0:T(512)S(1)} %add_rsqrt_fusion), kind=kOutput, calls=%fused_computation.41 | convolution fusion | flops 4847566848 | bytes 12588032 | tf_op jit(solution)/shard_map/dot_general | solution.py:92
  (47 shorter events, 13.2 us)
Async XLA Ops:
  6.5 165.1 %all-gather.3.cloned.1.call-start = ((), (), s32[]{:S(2)}) async-start(), calls=%async_computation.4 | async-start | bytes 5013504 | tf_op jit(solution)/shard_map/all_gather | solution.py:89
  10.8 35.4 %all-to-all-start.1 = ((f16[16,4,48,128]{3,2,1,0:T(8,128)(2,1)}), f16[16,4,48,128]{3,2,1,0:T(8,128)(2,1)S(1)}, u32[]{:S(2)}, u32[]{:S(2)}) async-start(f16[16,4,48,128]{3,2,1,0:T(8,128)(2,1)} %bitcast.59), calls=%async_computation.1 | async-start | bytes 1572864 | tf_op jit(solution)/shard_map/all_to_all | solution.py:39
  18.2 153.5 %all-gather.5.cloned.1.call-start = ((), (), s32[]{:S(2)}) async-start(), calls=%async_computation.5 | async-start | bytes 5013504 | tf_op jit(solution)/shard_map/all_gather | solution.py:93
  21.4 30.5 %copy-start = (f32[512,768]{1,0:T(8,128)S(1)}, f32[512,768]{1,0:T(8,128)}, u32[]{:S(2)}) copy-start(f32[512,768]{1,0:T(8,128)} %param.13) | copy-start | bytes 4718596
  46.2 5.9 %copy-start.8 = (f32[768]{0:T(1024)S(1)}, f32[768]{0:T(1024)}, u32[]{:S(2)}) copy-start(f32[768]{0:T(1024)} %param.16) | copy-start | bytes 9220
  46.2 36.4 %all-to-all-start.2 = ((f16[16,4,48,128]{3,2,1,0:T(8,128)(2,1)}), f16[16,4,48,128]{3,2,1,0:T(8,128)(2,1)}, u32[]{:S(2)}, u32[]{:S(2)}) async-start(f16[16,4,48,128]{3,2,1,0:T(8,128)(2,1)} %bitcast.58), calls=%async_computation.2 | async-start | bytes 1572864 | tf_op jit(solution)/shard_map/all_to_all | solution.py:39
  82.7 34.4 %all-to-all-start = ((f16[16,4,48,128]{3,1,2,0:T(4,128)(2,1)}), f16[16,4,48,128]{3,1,2,0:T(4,128)(2,1)}, u32[]{:S(2)}, u32[]{:S(2)}) async-start(f16[16,4,48,128]{3,1,2,0:T(4,128)(2,1)} %bitcast.1), calls=%async_computation | async-start | bytes 1572864 | tf_op jit(solution)/shard_map/all_to_all | solution.py:39
  107.4 11.3 %copy-start.7 = (f32[128,64,1]{0,1,2:T(8,128)S(1)}, f32[128,64,1]{0,1,2:T(8,128)}, u32[]{:S(2)}) copy-start(f32[128,64,1]{0,1,2:T(8,128)} %constant.41) | copy-start | bytes 98308
  118.7 1.5 copy-start.4
  118.7 1.5 copy-start.5
  120.9 1.0 copy-start.3
  121.8 3.0 %copy-start.1 = (f32[48,128,64]{1,0,2:T(8,128)S(1)}, f32[48,128,64]{1,0,2:T(8,128)}, u32[]{:S(2)}) copy-start(f32[48,128,64]{1,0,2:T(8,128)} %copy.44) | copy-start | bytes 4718596
  125.2 1.0 copy-start.2
  129.2 0.8 copy-start.6
  169.5 2.2 %copy-start.9 = (f32[768]{0:T(1024)S(1)}, f32[768]{0:T(1024)}, u32[]{:S(2)}) copy-start(f32[768]{0:T(1024)} %param.17) | copy-start | bytes 9220
Sparse Core Ops, SparseCore 0:
  9.6 81.1 all-gather.2
  93.1 70.7 all-gather.4

commit v2 on v1

--- a/solution.py
+++ b/solution.py
@@ -1,12 +1,17 @@
+import functools
+
 import jax
 import jax.numpy as jnp
 import numpy as np
 from jax import lax
+from jax.experimental import pallas as pl
+from jax.experimental.pallas import tpu as pltpu
 from jax.sharding import PartitionSpec as P
 
 LANES = 128
 EPSILON = 1e-06
 LINK = jnp.float16
+FILTER_LINK = jnp.bfloat16
 CONV_SCALE = 0.125
 
 
@@ -24,6 +29,224 @@
     return jnp.einsum(
         pattern, left, right, precision=lax.Precision.HIGH, preferred_element_type=jnp.float32
     )
+
+
+def remote(source, target, send, recv, where):
+    return pltpu.make_async_remote_copy(
+        src_ref=source,
+        dst_ref=target,
+        send_sem=send,
+        recv_sem=recv,
+        device_id=where,
+        device_id_type=pl.DeviceIdType.MESH,
+    )
+
+
+def greet(shards, groups):
+    me = lax.axis_index("sa")
+    barrier = pltpu.get_barrier_semaphore()
+
+    @pl.loop(1, shards)
+    def _(step):
+        pl.semaphore_signal(
+            barrier,
+            inc=1,
+            device_id={"sa": lax.rem(me + step, shards)},
+            device_id_type=pl.DeviceIdType.MESH,
+        )
+
+    for step in range(1, groups):
+        pl.semaphore_signal(
+            barrier,
+            inc=1,
+            device_id={"grp": lax.rem(lax.axis_index("grp") + step, groups)},
+            device_id_type=pl.DeviceIdType.MESH,
+        )
+    pl.semaphore_wait(barrier, shards + groups - 2)
+
+
+def scatter_copy(shards, number, step, source, target, send, recv):
+    me = lax.axis_index("sa")
+    to = lax.rem(me + step, shards)
+    return remote(
+        source.at[to], target.at[me], send.at[number, step], recv.at[number, step], {"sa": to}
+    )
+
+
+def start_scatter(shards, number, source, target, send, recv, local):
+    me = lax.axis_index("sa")
+    pltpu.make_async_copy(source.at[me], target.at[me], local.at[number]).start()
+
+    @pl.loop(1, shards)
+    def _(step):
+        scatter_copy(shards, number, step, source, target, send, recv).start()
+
+
+def finish_scatter(shards, number, source, target, send, recv, local):
+    me = lax.axis_index("sa")
+
+    @pl.loop(1, shards)
+    def _(step):
+        origin = lax.rem(me - step + shards, shards)
+        remote(
+            source.at[lax.rem(me + step, shards)],
+            target.at[origin],
+            send.at[number, step],
+            recv.at[number, step],
+            {"sa": lax.rem(me + step, shards)},
+        ).wait()
+
+    pltpu.make_async_copy(source.at[me], target.at[me], local.at[number]).wait()
+
+
+def exchange_kernel(
+    shards, groups, outer, inner, *refs
+):
+    sources, weights, targets, tables = refs[:2], refs[2:4], refs[4:6], refs[6:8]
+    send, recv, local, own, z_send, z_recv, x_send, x_recv, y_send, y_recv, c_send, c_recv = refs[8:]
+    me = lax.axis_index("sa")
+    group = lax.axis_index("grp")
+    core = lax.rem(me, 2)
+    mid = lax.rem(me // 2, inner)
+    far = me // (2 * inner)
+    place = lambda o, m, c: (o * inner + m) * 2 + c
+
+    def share(array, index):
+        width = array.shape[-1] // groups
+        return pl.ds(pl.multiple_of(index * width, 128), width)
+
+    def z_copy(a, o_to, o_own):
+        slot = place(o_own, mid, core)
+        part = share(tables[a], group)
+        return remote(
+            weights[a].at[:, part],
+            tables[a].at[slot, :, part],
+            z_send.at[a, o_to],
+            z_recv.at[a, o_own],
+            {"sa": place(o_to, mid, core)},
+        )
+
+    def x_copy(a, o_own, index):
+        slot = place(o_own, mid, core)
+        part = tables[a].at[slot, :, share(tables[a], index)]
+        other = lax.rem(group + 1, groups)
+        return remote(part, part, x_send.at[a, o_own], x_recv.at[a, o_own], {"grp": other})
+
+    def y_copy(a, o_own, step, m_own):
+        slot = place(o_own, m_own, core)
+        to = place(far, lax.rem(mid + step, inner), core)
+        entry = tables[a].at[slot]
+        return remote(entry, entry, y_send.at[a, step, o_own], y_recv.at[a, slot], {"sa": to})
+
+    def c_copy(a, o_own, m_own, c_own):
+        slot = place(o_own, m_own, c_own)
+        row = o_own * inner + m_own
+        entry = tables[a].at[slot]
+        return remote(
+            entry, entry, c_send.at[a, row], c_recv.at[a, row], {"sa": place(far, mid, 1 - core)}
+        )
+
+    def forward_y(a, o_own):
+        @pl.loop(1, inner)
+        def _(step):
+            y_copy(a, o_own, step, mid).start()
+
+        c_copy(a, o_own, mid, core).start()
+
+    greet(shards, groups)
+    for a in range(2):
+        pltpu.make_async_copy(weights[a], tables[a].at[me], own.at[a]).start()
+
+        @pl.loop(1, outer)
+        def _(step):
+            z_copy(a, lax.rem(far + step, outer), far).start()
+
+    for number in range(2):
+        start_scatter(shards, number, sources[number], targets[number], send, recv, local)
+    for a in range(2):
+        pltpu.make_async_copy(weights[a], tables[a].at[me], own.at[a]).wait()
+        forward_y(a, far)
+    for a in range(2):
+        @pl.loop(1, outer)
+        def _(step):
+            origin = lax.rem(far - step + outer, outer)
+            z_copy(a, far, origin).wait_recv()
+            x_copy(a, origin, group).start()
+
+    for a in range(2):
+        @pl.loop(1, outer)
+        def _(step):
+            origin = lax.rem(far - step + outer, outer)
+            x_copy(a, origin, lax.rem(group + 1, groups)).wait_recv()
+            forward_y(a, origin)
+
+    for a in range(2):
+        @pl.loop(0, outer)
+        def _(turn):
+            origin = lax.rem(far - turn + outer, outer)
+
+            @pl.loop(1, inner)
+            def _(step):
+                m_own = lax.rem(mid - step + inner, inner)
+                y_copy(a, origin, step, m_own).wait_recv()
+                c_copy(a, origin, m_own, core).start()
+
+    for number in range(2):
+        finish_scatter(shards, number, sources[number], targets[number], send, recv, local)
+    for a in range(2):
+        @pl.loop(0, outer)
+        def _(o_own):
+            @pl.loop(0, inner)
+            def _(m_own):
+                c_copy(a, o_own, m_own, 1 - core).wait_recv()
+                c_copy(a, o_own, m_own, core).wait_send()
+
+            @pl.loop(1, inner)
+            def _(step):
+                y_copy(a, o_own, step, mid).wait_send()
+
+        @pl.loop(1, outer)
+        def _(step):
+            origin = lax.rem(far - step + outer, outer)
+            x_copy(a, origin, group).wait_send()
+            z_copy(a, lax.rem(far + step, outer), far).wait_send()
+
+
+def anywhere(count):
+    return [pl.BlockSpec(memory_space=pl.ANY)] * count
+
+
+def exchange(packed, w_in, w_out):
+    shards, groups = lax.axis_size("sa"), lax.axis_size("grp")
+    inner = 1
+    while inner * inner * 4 <= shards // 2:
+        inner *= 2
+    outer = shards // (2 * inner)
+    dma = pltpu.SemaphoreType.DMA
+    shapes = [jax.ShapeDtypeStruct(v.shape, v.dtype) for v in packed] + [
+        jax.ShapeDtypeStruct((shards,) + w.shape, w.dtype) for w in (w_in, w_out)
+    ]
+    return pl.pallas_call(
+        functools.partial(exchange_kernel, shards, groups, outer, inner),
+        out_shape=shapes,
+        in_specs=anywhere(4),
+        out_specs=anywhere(4),
+        scratch_shapes=[
+            dma((2, shards)),
+            dma((2, shards)),
+            dma((2,)),
+            dma((2,)),
+            dma((2, outer)),
+            dma((2, outer)),
+            dma((2, outer)),
+            dma((2, outer)),
+            dma((2, inner, outer)),
+            dma((2, shards)),
+            dma((2, outer * inner)),
+            dma((2, outer * inner)),
+        ],
+        compiler_params=pltpu.CompilerParams(collective_id=1, has_side_effects=True),
+    )(*packed, w_in, w_out)
 
 
 def on_device(tokens, kernel_re, kernel_im, mix_gain, mlp_gain, w_in, w_out):
@@ -34,20 +257,25 @@
     total = shards * rows
     outer = total // LANES
 
-    def to_channels(values):
-        packed = values.astype(LINK).reshape(blocks, LANES, shards, part).transpose(2, 0, 3, 1)
-        moved = lax.all_to_all(packed, "sa", split_axis=0, concat_axis=0, tiled=True)
-        return moved.reshape(outer, part, LANES)
+    def pack(values, link):
+        return values.astype(link).reshape(blocks, LANES, shards, part).transpose(2, 0, 3, 1)
 
     normed = rms_scale(tokens) * mix_gain
-    signal = to_channels(normed).astype(jnp.float32)
-
-    def by_frequency(moved):
-        ordered = moved.transpose(1, 0, 2).reshape(part, LANES, outer)
+    signal = lax.all_to_all(pack(normed, LINK), "sa", split_axis=0, concat_axis=0, tiled=True)
+    signal = signal.reshape(outer, part, LANES).astype(jnp.float32)
+    *moved, w_in, w_out = exchange(
+        [pack(kernel_re, FILTER_LINK), pack(kernel_im, FILTER_LINK)], w_in, w_out
+    )
+    moved = [values.reshape(outer, part, LANES) for values in moved]
+    w_in = w_in.reshape(channels, -1)
+    w_out = w_out.reshape(-1, channels)
+
+    def by_frequency(values):
+        ordered = values.transpose(1, 0, 2).reshape(part, LANES, outer)
         return ordered.transpose(2, 0, 1).astype(jnp.float32)
 
-    filter_re = by_frequency(to_channels(kernel_re))
-    filter_im = by_frequency(to_channels(kernel_im))
+    filter_re = by_frequency(moved[0])
+    filter_im = by_frequency(moved[1])
 
     cos_outer, sin_outer = angles(outer, outer, outer)
     cos_inner, sin_inner = angles(LANES, LANES, LANES)
@@ -86,11 +314,11 @@
     mixed = tokens + conv * jax.nn.sigmoid(normed)
     scaled = (rms_scale(mixed) * mlp_gain).astype(jnp.bfloat16)
     hidden_pre = jnp.dot(
-        scaled, lax.all_gather(w_in, "sa", axis=0, tiled=True), preferred_element_type=jnp.float32
+        scaled, w_in, preferred_element_type=jnp.float32
     )
     hidden = jax.nn.gelu(hidden_pre, approximate=True).astype(jnp.bfloat16)
     branch = jnp.dot(
-        hidden, lax.all_gather(w_out, "sa", axis=0, tiled=True), preferred_element_type=jnp.float32
+        hidden, w_out, preferred_element_type=jnp.float32
     )
     return mixed + branch
 

time: 190 us -> 192 us (1.011)
  Pallas kernels: 0 us -> 102 us
  waiting for transfers between devices: 61.2 us -> 0.01 us
  starting transfers between devices: 23.3 us -> 7.35 us
  between operations: 13.7 us -> 0.26 us
  blocking collectives: 36 us -> 26.6 us
    pallas_call x0 -> x1, Pallas kernels: none -> 102 us  [exchange(): pl.pallas_call(functools.partial(exchange_kernel, shards, groups, outer,...]
    all_to_all x3 -> x1, waiting for transfers between devices: 59.8 us -> 0.01 us  [on_device(): lax.all_to_all(pack(normed, LINK), 'sa', split_axis=0, concat_axis=0, til...]
    all_to_all x3 -> x1, starting transfers between devices: 23.2 us -> 7.35 us  [on_device(): lax.all_to_all(pack(normed, LINK), 'sa', split_axis=0, concat_axis=0, til...]
    all_to_all x1, blocking collectives: 36 us -> 26.6 us  [on_device(): conv = lax.all_to_all(conv, 'sa', split_axis=0, concat_axis=0, tiled=True)]
    convert_element_type x3, other arithmetic: 4.19 us -> 1.81 us  [pack(): values.astype(link).reshape(blocks, LANES, shards, part)]
    convert_element_type x3, local copies, waits for them, and re-layouts: 3.16 us -> 1.23 us  [pack(): values.astype(link).reshape(blocks, LANES, shards, part)]
  transfers between devices with their start and end apart: 5 -> 1, of which waited for: 3 -> 0; matrix products, arithmetic and copies ran while one was open for 23% -> 11% of each run, Pallas kernels for 0% -> 53%
where the time goes in v2:
time: 192 us
  Pallas kernels  102 us (53%)
  blocking collectives  26.6 us (14%)
  local copies, waits for them, and re-layouts  25.5 us (13%)
  matrix products  18.8 us (10%)
  other arithmetic  10.8 us (6%)
  starting transfers between devices  7.35 us (4%)
    pallas_call x1, Pallas kernels, exchange(): pl.pallas_call(functools.partial(exchange_kernel, shards, groups, outer,...  102 us
    all_to_all x1, blocking collectives, on_device(): conv = lax.all_to_all(conv, 'sa', split_axis=0, concat_axis=0, tiled=True)  26.6 us
    convert_element_type x6, local copies, waits for them, and re-layouts, by_frequency(): return ordered.transpose(2, 0, 1).astype(jnp.float32)  14.5 us
    dot_general x1, matrix products, on_device(): branch = jnp.dot(hidden, w_out, preferred_element_type=jnp.float32)  10.3 us
    dot_general x4, matrix products, contract(): jnp.einsum(pattern, left, right, precision=lax.Precision.HIGH, preferred_...  8.5 us
    all_to_all x1, starting transfers between devices, on_device(): lax.all_to_all(pack(normed, LINK), 'sa', split_axis=0, concat_axis=0, til...  7.35 us
  transfers between devices with their start and end apart: 1, of which 0 were waited for; matrix products, arithmetic and copies ran while one was open for 11% of the time, Pallas kernels for 53%

profile of v2, /device:TPU:1, one launch (start us, length us, event | category | flops | bytes accessed | tf_op | source)
XLA Modules:
  0.0 191.7 jit_solution(13515138826252449656)
XLA Ops:
  0.0 1.7 multiply_reduce_fusion.1
  2.8 1.1 reshape.55
  4.0 7.3 %all-to-all-start = ((f16[16,4,48,128]{3,1,2,0:T(4,128)(2,1)}), f16[16,4,48,128]{3,1,2,0:T(4,128)(2,1)}, u32[]{:S(2)}, u32[]{:S(2)}) async-start(f16[16,4,48,128]{3,1,2,0:T(4,128)(2,1)} %bitcast.1), calls=%async_computation | async-start | bytes 1572864 | tf_op jit(solution)/shard_map/all_to_all | solution.py:264
  11.3 1.5 convert_element_type.58
  13.3 1.0 copy.50
  15.5 1.0 copy.49
  16.6 102.4 %shard_map.127 = (bf16[16,4,48,128]{3,2,1,0:T(8,128)(2,1)}, bf16[16,4,48,128]{3,2,1,0:T(8,128)(2,1)}, bf16[16,48,3072]{2,1,0:T(8,128)(2,1)}, bf16[16,192,768]{2,1,0:T(8,128)(2,1)}) custom-call(bf16[16,4,48,128]{3,2,1,0:T(8,128)(2,1)} %bitcast.68, bf16[16,4,48,128]{3,2,1,0:T(8,128)(2,1)} %bitcast.69, bf16[48,3072]{1,0:T(8,128)(2,1)} %refs_2_.1, ...), custom_call_target="tpu_custom_call" | custom-call | tf_op jit(solution)/shard_map/pallas_call | solution.py:229
  119.0 2.7 %bitcast_convert_fusion = (f32[64,48,128]{2,1,0:T(8,128)S(1)}, f32[64,48,128]{2,1,0:T(8,128)}) fusion(bf16[16,4,48,128]{3,2,1,0:T(8,128)(2,1)} %get-tuple-element.10, bf16[16,4,48,128]{3,2,1,0:T(8,128)(2,1)} %get-tuple-element.9), kind=kLoop, calls=%fused_computation.43 | loop fusion | flops 786432 | bytes 4718592 | tf_op jit(solution)/shard_map/convert_element_type | solution.py:275
  122.2 2.0 %reshape.63 = f32[48,128,64]{2,1,0:T(8,128)} reshape(f32[48,64,128]{2,1,0:T(8,128)S(1)} %bitcast.66) | data formatting | bytes 3145728 | tf_op jit(solution)/shard_map/convert_element_type | solution.py:275
  124.2 2.4 %copy.29 = f32[48,128,64]{1,0,2:T(8,128)S(1)} copy(f32[48,128,64]{2,1,0:T(8,128)} %reshape.63) | data formatting | bytes 3145728 | tf_op jit(solution)/shard_map/convert_element_type | solution.py:275
  126.6 3.1 %copy.48 = f32[64,48,128]{2,0,1:T(8,128)} copy(f32[64,48,128]{2,1,0:T(8,128)} %get-tuple-element.22) | data formatting | bytes 3145728 | tf_op jit(solution)/shard_map/convert_element_type | solution.py:275
  129.7 3.3 %reshape.62 = f32[48,128,64]{2,1,0:T(8,128)} reshape(f32[48,64,128]{2,1,0:T(8,128)} %bitcast.67) | data formatting | bytes 3145728 | tf_op jit(solution)/shard_map/convert_element_type | solution.py:275
  133.1 3.2 %copy.27 = f32[48,128,64]{1,0,2:T(8,128)} copy(f32[48,128,64]{2,1,0:T(8,128)} %reshape.62) | data formatting | bytes 3145728 | tf_op jit(solution)/shard_map/convert_element_type | solution.py:275
  136.3 1.6 copy.20
  137.9 1.5 fusion.36
  139.4 0.7 multiply_add_fusion.2
  141.0 3.0 %fusion.14 = f32[64,48,256]{2,1,0:T(8,128)S(1)} fusion(f32[256,256,1]{1,0,2:T(8,128)S(1)} %copy-done.4, f32[64,48,256]{2,0,1:T(8,128)S(1)} %pad_maximum_fusion), kind=kOutput, calls=%fused_computation.17 | convolution fusion | flops 1207959552 | bytes 6553600 | tf_op jit(solution)/shard_map/cdb,be->cde/dot_general | solution.py:29
  144.7 0.7 copy-done.3
  145.4 3.0 %fusion.12 = f32[64,48,256]{2,0,1:T(8,128)S(1)} fusion(f32[256,256,1]{1,0,2:T(8,128)S(1)} %copy-done.3, f32[64,48,256]{2,1,0:T(8,128)S(1)} %pad_maximum_fusion.1), kind=kOutput, calls=%fused_computation.15 | convolution fusion | flops 1207959552 | bytes 6553600 | tf_op jit(solution)/shard_map/cde,eb->cdb/dot_general | solution.py:29
  149.2 1.0 multiply_convert_fusion.1
  150.6 26.6 %all_to_all.10 = f16[16,4,48,128]{3,1,2,0:T(4,128)(2,1)S(1)} all-to-all(f16[16,4,48,128]{3,1,2,0:T(4,128)(2,1)S(1)} %copy.32), channel_id=1, replica_groups=mesh['grp'=2,'sa'=16] {'sa'}, dimensions={0} | all-to-all | bytes 1572864 | tf_op jit(solution)/shard_map/all_to_all | solution.py:311
  177.7 1.6 copy.33
  179.3 2.1 %multiply_reduce_fusion = (f32[512]{0:T(512)S(1)}, f32[512,768]{1,0:T(8,128)S(1)}) fusion(f32[512,768]{1,0:T(8,128)S(1)} %copy-done, f32[512,768]{1,0:T(8,128)} %copy.33, f32[768]{0:T(1024)S(1)} %copy-done.9, f32[512]{0:T(512)S(1)} %add_rsqrt_fusion.1), kind=kLoop, calls=%fused_computation.30 | loop fusion | flops 3538432 | bytes 4725760 | tf_op jit(solution)/shard_map/reduce_sum | solution.py:19
  181.4 10.3 %fusion.23 = f32[512,768]{1,0:T(8,128)} fusion(f32[512,768]{1,0:T(8,128)S(1)} %get-tuple-element.14, bf16[3072,768]{1,0:T(8,128)(2,1)} %bitcast.73, bf16[768,3072]{1,0:T(8,128)(2,1)} %bitcast.72, f32[768]{0:T(1024)S(1)} %copy-done.10, f32[512]{0:T(512)S(1)} %add_rsqrt_fusion), kind=kOutput, calls=%fused_computation.41 | convolution fusion | flops 4847566848 | bytes 12588032 | tf_op jit(solution)/shard_map/dot_general | solution.py:320
  (39 shorter events, 6.5 us)
Async XLA Ops:
  0.0 1.9 copy-start
  0.0 1.9 copy-start.9
  4.0 132.3 %all-to-all-start = ((f16[16,4,48,128]{3,1,2,0:T(4,128)(2,1)}), f16[16,4,48,128]{3,1,2,0:T(4,128)(2,1)}, u32[]{:S(2)}, u32[]{:S(2)}) async-start(f16[16,4,48,128]{3,1,2,0:T(4,128)(2,1)} %bitcast.1), calls=%async_computation | async-start | bytes 1572864 | tf_op jit(solution)/shard_map/all_to_all | solution.py:264
  13.3 1.7 copy-start.2
  136.3 1.6 copy-start.8
  137.9 1.5 copy-start.5
  137.9 1.5 copy-start.6
  140.1 1.0 copy-start.4
  141.0 3.0 %copy-start.1 = (f32[48,128,64]{1,0,2:T(8,128)S(1)}, f32[48,128,64]{1,0,2:T(8,128)}, u32[]{:S(2)}) copy-start(f32[48,128,64]{1,0,2:T(8,128)} %copy.27) | copy-start | bytes 4718596
  144.4 1.0 copy-start.3
  148.4 0.8 copy-start.7
  179.3 2.1 %copy-start.10 = (f32[768]{0:T(1024)S(1)}, f32[768]{0:T(1024)}, u32[]{:S(2)}) copy-start(f32[768]{0:T(1024)} %param.17) | copy-start | bytes 9220

commit v3 on v1

--- a/solution.py
+++ b/solution.py
@@ -26,6 +26,16 @@
     )
 
 
+def half_of(weights, group):
+    width = weights.shape[1] // 2
+    return jnp.where(group == 0, weights[:, :width], weights[:, width:])
+
+
+def join(mine, other, group):
+    left = jnp.where(group == 0, mine, other)
+    return jnp.concatenate([left, jnp.where(group == 0, other, mine)], 1)
+
+
 def on_device(tokens, kernel_re, kernel_im, mix_gain, mlp_gain, w_in, w_out):
     shards = lax.axis_size("sa")
     rows, channels = tokens.shape
@@ -34,20 +44,35 @@
     total = shards * rows
     outer = total // LANES
 
-    def to_channels(values):
-        packed = values.astype(LINK).reshape(blocks, LANES, shards, part).transpose(2, 0, 3, 1)
+    def pack(values):
+        return values.astype(LINK).reshape(blocks, LANES, shards, part).transpose(2, 0, 3, 1)
+
+    def to_channels(packed):
         moved = lax.all_to_all(packed, "sa", split_axis=0, concat_axis=0, tiled=True)
         return moved.reshape(outer, part, LANES)
 
+    group = lax.axis_index("grp")
+    swap = [(0, 1), (1, 0)]
+    in_mine = lax.all_gather(half_of(w_in, group), "sa", axis=0, tiled=True)
+    packed_im, out_half, in_mine = lax.optimization_barrier(
+        (pack(kernel_im), half_of(w_out, group), in_mine)
+    )
+    in_other = lax.ppermute(in_mine, "grp", swap)
+    out_mine = lax.all_gather(out_half, "sa", axis=0, tiled=True)
+
     normed = rms_scale(tokens) * mix_gain
-    signal = to_channels(normed).astype(jnp.float32)
+    packed_re = pack(kernel_re)
+    moved_re = to_channels(packed_re)
+    packed_normed, out_mine = lax.optimization_barrier((pack(normed), out_mine))
+    out_other = lax.ppermute(out_mine, "grp", swap)
+    signal = to_channels(packed_normed).astype(jnp.float32)
 
     def by_frequency(moved):
         ordered = moved.transpose(1, 0, 2).reshape(part, LANES, outer)
         return ordered.transpose(2, 0, 1).astype(jnp.float32)
 
-    filter_re = by_frequency(to_channels(kernel_re))
-    filter_im = by_frequency(to_channels(kernel_im))
+    filter_re = by_frequency(moved_re)
+    filter_im = by_frequency(to_channels(packed_im))
 
     cos_outer, sin_outer = angles(outer, outer, outer)
     cos_inner, sin_inner = angles(LANES, LANES, LANES)
@@ -80,17 +105,18 @@
     )
     conv = contract("ac,cdb->adb", last, untwisted)
     conv = (conv * (CONV_SCALE / total)).astype(LINK).reshape(shards, blocks, part, LANES)
+    conv, in_other = lax.optimization_barrier((conv, in_other))
     conv = lax.all_to_all(conv, "sa", split_axis=0, concat_axis=0, tiled=True)
     conv = conv.transpose(1, 3, 0, 2).reshape(rows, channels).astype(jnp.float32) * (1 / CONV_SCALE)
 
     mixed = tokens + conv * jax.nn.sigmoid(normed)
     scaled = (rms_scale(mixed) * mlp_gain).astype(jnp.bfloat16)
     hidden_pre = jnp.dot(
-        scaled, lax.all_gather(w_in, "sa", axis=0, tiled=True), preferred_element_type=jnp.float32
+        scaled, join(in_mine, in_other, group), preferred_element_type=jnp.float32
     )
     hidden = jax.nn.gelu(hidden_pre, approximate=True).astype(jnp.bfloat16)
     branch = jnp.dot(
-        hidden, lax.all_gather(w_out, "sa", axis=0, tiled=True), preferred_element_type=jnp.float32
+        hidden, join(out_mine, out_other, group), preferred_element_type=jnp.float32
     )
     return mixed + branch
 

time: 190 us -> 255 us (1.34)
  waiting for transfers between devices: 61.2 us -> 127 us
  other arithmetic: 10.3 us -> 20.5 us
  blocking collectives: 36 us -> 29.1 us
  starting transfers between devices: 23.3 us -> 18.5 us
    ppermute x0 -> x2, waiting for transfers between devices: none -> 62.4 us  [the longest x1 36.8 us: on_device(): out_other = lax.ppermute(out_mine, 'grp', swap)]
    all_gather x2, waiting for transfers between devices: 0.04 us -> 60.8 us  [the longest x1 41.8 us: on_device(): in_mine = lax.all_gather(half_of(w_in, group), 'sa', axis=0, tiled=True)]
    all_to_all x3 -> x2, waiting for transfers between devices: 59.8 us -> 3.68 us  [to_channels(): lax.all_to_all(packed, 'sa', split_axis=0, concat_axis=0, tiled=True)]
    all_to_all x3 -> x2, starting transfers between devices: 23.2 us -> 9.55 us  [to_channels(): lax.all_to_all(packed, 'sa', split_axis=0, concat_axis=0, tiled=True)]
    select_n x0 -> x4, other arithmetic: none -> 11.6 us  [the longest x2 9.3 us: join(): left = jnp.where(group == 0, mine, other)]
    all_to_all x0 -> x1, starting transfers between devices: none -> 7.41 us  [on_device(): conv = lax.all_to_all(conv, 'sa', split_axis=0, concat_axis=0, tiled=True)]
    all_to_all x1, blocking collectives: 36 us -> 29.1 us  [to_channels(): lax.all_to_all(packed, 'sa', split_axis=0, concat_axis=0, tiled=True)]
  transfers between devices with their start and end apart: 5 -> 7, of which waited for: 3 -> 6; matrix products, arithmetic and copies ran while one was open for 23% -> 19% of each run, Pallas kernels for 0% -> 0%
where the time goes in v3:
time: 255 us; the launch traced here: 253 us
  waiting for transfers between devices  127 us (50%)
  blocking collectives  29.1 us (11%)
  local copies, waits for them, and re-layouts  25.5 us (10%)
  other arithmetic  20.5 us (8%)
  matrix products  18.7 us (7%)
  starting transfers between devices  18.5 us (7%)
  between operations  13.7 us (5%)
    all_gather x1, waiting for transfers between devices, on_device(): in_mine = lax.all_gather(half_of(w_in, group), 'sa', axis=0, tiled=True)  41.8 us
    ppermute x1, waiting for transfers between devices, on_device(): out_other = lax.ppermute(out_mine, 'grp', swap)  36.8 us
    all_to_all x1, blocking collectives, to_channels(): lax.all_to_all(packed, 'sa', split_axis=0, concat_axis=0, tiled=True)  29.1 us
    ppermute x1, waiting for transfers between devices, on_device(): in_other = lax.ppermute(in_mine, 'grp', swap)  25.6 us
    all_gather x1, waiting for transfers between devices, on_device(): out_mine = lax.all_gather(out_half, 'sa', axis=0, tiled=True)  18.9 us
    convert_element_type x6, local copies, waits for them, and re-layouts, by_frequency(): return ordered.transpose(2, 0, 1).astype(jnp.float32)  13 us
    dot_general x1, matrix products, on_device(): jnp.dot(hidden, join(out_mine, out_other, group), preferred_element_type=...  10.2 us
    all_to_all x2, starting transfers between devices, to_channels(): lax.all_to_all(packed, 'sa', split_axis=0, concat_axis=0, tiled=True)  9.55 us
  transfers between devices with their start and end apart: 7, of which 6 were waited for; matrix products, arithmetic and copies ran while one was open for 19% of the time, Pallas kernels for 0%

profile of v3, /device:TPU:1, one launch (start us, length us, event | category | flops | bytes accessed | tf_op | source)
XLA Modules:
  0.0 252.9 jit_solution(7366008946362241717)
XLA Ops:
  6.5 1.7 slice_select_fusion
  12.6 41.8 %all-gather.3.cloned.1.call-done = bf16[768,1536]{1,0:T(8,128)(2,1)} async-done(((bf16[48,1536]{1,0:T(8,128)(2,1)}), bf16[768,1536]{1,0:T(8,128)(2,1)}) %all-gather.3.cloned.1.call-update) | async-done | bytes 2359312 | tf_op jit(solution)/shard_map/all_gather | solution.py:56
  55.7 29.1 %all_to_all.20 = f16[16,4,48,128]{3,2,1,0:T(8,128)(2,1)} all-to-all(f16[16,4,48,128]{3,2,1,0:T(8,128)(2,1)S(1)} %bitcast.60), channel_id=1, replica_groups=mesh['grp'=2,'sa'=16] {'sa'}, dimensions={0} | all-to-all | bytes 1572864 | tf_op jit(solution)/shard_map/all_to_all | solution.py:51
  84.8 3.7 %all-to-all-start.2 = ((f16[16,4,48,128]{3,2,1,0:T(8,128)(2,1)}), f16[16,4,48,128]{3,2,1,0:T(8,128)(2,1)S(1)}, u32[]{:S(2)}, u32[]{:S(2)}) async-start(f16[16,4,48,128]{3,2,1,0:T(8,128)(2,1)} %bitcast.57), calls=%async_computation.2 | async-start | bytes 1572864 | tf_op jit(solution)/shard_map/all_to_all | solution.py:51
  89.8 1.8 copy.34
  92.8 18.9 %all-gather.5.cloned.1.call-done = bf16[3072,384]{1,0:T(8,128)(2,1)} async-done(((bf16[192,384]{1,0:T(8,128)(2,1)}), bf16[3072,384]{1,0:T(8,128)(2,1)}) %all-gather.5.cloned.1.call-update) | async-done | bytes 2359312 | tf_op jit(solution)/shard_map/all_gather | solution.py:61
  112.7 5.9 %all-to-all-start = ((f16[16,4,48,128]{3,1,2,0:T(4,128)(2,1)}), f16[16,4,48,128]{3,1,2,0:T(4,128)(2,1)}, u32[]{:S(2)}, u32[]{:S(2)}) async-start(f16[16,4,48,128]{3,1,2,0:T(4,128)(2,1)} %bitcast.1), calls=%async_computation | async-start | bytes 1572864 | tf_op jit(solution)/shard_map/all_to_all | solution.py:51
  119.3 1.9 reshape.54
  121.3 2.4 copy.42
  126.2 1.6 copy.43
  127.9 3.3 %reshape.55 = f32[48,128,64]{2,1,0:T(8,128)} reshape(f32[48,64,128]{2,1,0:T(8,128)} %copy.43) | data formatting | bytes 3145728 | tf_op jit(solution)/shard_map/convert_element_type | solution.py:72
  131.2 3.2 %copy.44 = f32[48,128,64]{1,0,2:T(8,128)} copy(f32[48,128,64]{2,1,0:T(8,128)} %reshape.55) | data formatting | bytes 3145728 | tf_op jit(solution)/shard_map/convert_element_type | solution.py:72
  134.6 2.6 %all-to-all-done = f16[16,4,48,128]{3,1,2,0:T(4,128)(2,1)} async-done(((f16[16,4,48,128]{3,1,2,0:T(4,128)(2,1)}), f16[16,4,48,128]{3,1,2,0:T(4,128)(2,1)}, u32[]{:S(2)}, u32[]{:S(2)}) %all-to-all-start) | async-done | bytes 786464 | tf_op jit(solution)/shard_map/all_to_all | solution.py:51
  137.3 1.6 copy.37
  142.0 3.0 %fusion.22 = f32[64,48,256]{2,1,0:T(8,128)S(1)} fusion(f32[256,256,1]{1,0,2:T(8,128)S(1)} %copy-done.8, f32[64,48,256]{2,0,1:T(8,128)S(1)} %pad_maximum_fusion), kind=kOutput, calls=%fused_computation.25 | convolution fusion | flops 1207959552 | bytes 6553600 | tf_op jit(solution)/shard_map/cdb,be->cde/dot_general | solution.py:24
  146.4 3.0 %fusion.20 = f32[64,48,256]{2,0,1:T(8,128)S(1)} fusion(f32[256,256,1]{1,0,2:T(8,128)S(1)} %copy-done.7, f32[64,48,256]{2,1,0:T(8,128)S(1)} %pad_maximum_fusion.1), kind=kOutput, calls=%fused_computation.23 | convolution fusion | flops 1207959552 | bytes 6553600 | tf_op jit(solution)/shard_map/cde,eb->cdb/dot_general | solution.py:24
  151.2 25.6 %collective-permute-done = bf16[768,1536]{1,0:T(8,128)(2,1)} collective-permute-done((bf16[768,1536]{1,0:T(8,128)(2,1)}, bf16[768,1536]{1,0:T(8,128)(2,1)}, u32[]{:S(2)}, u32[]{:S(2)}) %collective-permute-start) | collective-permute-done | bytes 2359328 | tf_op jit(solution)/shard_map/ppermute | solution.py:60
  178.0 7.4 %all-to-all-start.3 = ((f16[16,4,48,128]{3,1,2,0:T(4,128)(2,1)}), f16[16,4,48,128]{3,1,2,0:T(4,128)(2,1)S(1)}, u32[]{:S(2)}, u32[]{:S(2)}) async-start(f16[16,4,48,128]{3,1,2,0:T(4,128)(2,1)} %copy.47), calls=%async_computation.3 | async-start | bytes 1572864 | tf_op jit(solution)/shard_map/all_to_all | solution.py:109
  185.5 5.0 %broadcast_select_fusion.3 = (bf16[768,1536]{1,0:T(8,128)(2,1)}, bf16[768,1536]{1,0:T(8,128)(2,1)}) fusion(bf16[768,1536]{1,0:T(8,128)(2,1)} %all-gather.3.cloned.1.call-done, bf16[768,1536]{1,0:T(8,128)(2,1)} %collective-permute-done, pred[]{:T(512)S(6)} %eq.2), kind=kLoop, calls=%fused_computation.33 | loop fusion | flops 2359296 | bytes 9437185 | tf_op jit(solution)/shard_map/jit(_where)/select_n | solution.py:35
  190.5 36.8 %collective-permute-done.1 = bf16[3072,384]{1,0:T(8,128)(2,1)} collective-permute-done((bf16[3072,384]{1,0:T(8,128)(2,1)}, bf16[3072,384]{1,0:T(8,128)(2,1)}, u32[]{:S(2)}, u32[]{:S(2)}) %collective-permute-start.1) | collective-permute-done | bytes 2359328 | tf_op jit(solution)/shard_map/ppermute | solution.py:67
  227.3 4.3 %broadcast_select_fusion.1 = (bf16[3072,384]{1,0:T(8,128)(2,1)}, bf16[3072,384]{1,0:T(8,128)(2,1)}) fusion(bf16[3072,384]{1,0:T(8,128)(2,1)S(1)} %copy-done.4, bf16[3072,384]{1,0:T(8,128)(2,1)} %collective-permute-done.1, pred[]{:T(512)S(6)} %eq.2), kind=kLoop, calls=%fused_computation.31 | loop fusion | flops 2359296 | bytes 9437185 | tf_op jit(solution)/shard_map/jit(_where)/select_n | solution.py:35
  232.1 1.6 copy.48
  233.8 2.1 multiply_reduce_fusion
  235.9 10.2 %fusion.33 = f32[512,768]{1,0:T(8,128)} fusion(f32[512,768]{1,0:T(8,128)S(1)} %get-tuple-element.20, bf16[3072,384]{1,0:T(8,128)(2,1)} %get-tuple-element.26, bf16[3072,384]{1,0:T(8,128)(2,1)} %get-tuple-element.25, bf16[768,1536]{1,0:T(8,128)(2,1)} %get-tuple-element.24, bf16[768,1536]{1,0:T(8,128)(2,1)} %get-tuple-element.23, f32[768]{0:T(1024)S(1)} %copy-done.14, ...), kind=kOutput, calls=%fused_computation.55 | convolution fusion | flops 4866441216 | bytes 12588032 | tf_op jit(solution)/shard_map/dot_general | solution.py:118
  (65 shorter events, 20.6 us)
Async XLA Ops:
  6.5 47.9 %all-gather.3.cloned.1.call-start = ((), (), s32[]{:S(2)}) async-start(), calls=%async_computation.4 | async-start | bytes 2506752 | tf_op jit(solution)/shard_map/all_gather | solution.py:56
  8.2 103.5 %all-gather.5.cloned.1.call-start = ((), (), s32[]{:S(2)}) async-start(), calls=%async_computation.5 | async-start | bytes 2506752 | tf_op jit(solution)/shard_map/all_gather | solution.py:61
  10.5 1.4 copy-start.6
  10.5 43.9 %copy-start.5 = (f32[512,768]{1,0:T(8,128)S(1)}, f32[512,768]{1,0:T(8,128)}, u32[]{:S(2)}) copy-start(f32[512,768]{1,0:T(8,128)} %param.14) | copy-start | bytes 4718596
  55.7 32.7 %copy-start = (f32[512,768]{1,0:T(8,128)S(1)}, f32[512,768]{1,0:T(8,128)}, u32[]{:S(2)}) copy-start(f32[512,768]{1,0:T(8,128)} %param.13) | copy-start | bytes 4718596
  84.8 3.9 %copy-start.13 = (f32[768]{0:T(1024)S(1)}, f32[768]{0:T(1024)}, u32[]{:S(2)}) copy-start(f32[768]{0:T(1024)} %param.16) | copy-start | bytes 9220
  84.8 28.0 %all-to-all-start.2 = ((f16[16,4,48,128]{3,2,1,0:T(8,128)(2,1)}), f16[16,4,48,128]{3,2,1,0:T(8,128)(2,1)S(1)}, u32[]{:S(2)}, u32[]{:S(2)}) async-start(f16[16,4,48,128]{3,2,1,0:T(8,128)(2,1)} %bitcast.57), calls=%async_computation.2 | async-start | bytes 1572864 | tf_op jit(solution)/shard_map/all_to_all | solution.py:51
  92.8 25.9 %copy-start.3 = (f16[16,4,48,128]{3,2,1,0:T(8,128)(2,1)S(1)}, f16[16,4,48,128]{3,2,1,0:T(8,128)(2,1)}, u32[]{:S(2)}) copy-start(f16[16,4,48,128]{3,2,1,0:T(8,128)(2,1)} %all_to_all.20) | copy-start | bytes 2359300
  112.7 5.9 %copy-start.2 = (f16[16,4,48,128]{3,2,1,0:T(8,128)(2,1)}, f16[16,4,48,128]{3,2,1,0:T(8,128)(2,1)S(1)}, u32[]{:S(2)}) copy-start(f16[16,4,48,128]{3,2,1,0:T(8,128)(2,1)S(1)} %all-to-all-done.2) | copy-start | bytes 2359300
  112.7 24.5 %all-to-all-start = ((f16[16,4,48,128]{3,1,2,0:T(4,128)(2,1)}), f16[16,4,48,128]{3,1,2,0:T(4,128)(2,1)}, u32[]{:S(2)}, u32[]{:S(2)}) async-start(f16[16,4,48,128]{3,1,2,0:T(4,128)(2,1)} %bitcast.1), calls=%async_computation | async-start | bytes 1572864 | tf_op jit(solution)/shard_map/all_to_all | solution.py:51
  123.7 53.1 %collective-permute-start = (bf16[768,1536]{1,0:T(8,128)(2,1)}, bf16[768,1536]{1,0:T(8,128)(2,1)}, u32[]{:S(2)}, u32[]{:S(2)}) collective-permute-start(bf16[768,1536]{1,0:T(8,128)(2,1)} %all-gather.3.cloned.1.call-done), channel_id=1, source_target_pairs={{0,16},{16,0},{1,17},{17,1},{2,18},{18,2},{3,19},{19,3},{4,20},{20... | collective-permute-start | bytes 7077896 | tf_op jit(solution)/shard_map/ppermute | solution.py:60
  134.4 4.5 %copy-start.12 = (f32[128,64,1]{0,1,2:T(8,128)S(1)}, f32[128,64,1]{0,1,2:T(8,128)}, u32[]{:S(2)}) copy-start(f32[128,64,1]{0,1,2:T(8,128)} %constant.49) | copy-start | bytes 98308
  134.4 92.9 %collective-permute-start.1 = (bf16[3072,384]{1,0:T(8,128)(2,1)}, bf16[3072,384]{1,0:T(8,128)(2,1)}, u32[]{:S(2)}, u32[]{:S(2)}) collective-permute-start(bf16[3072,384]{1,0:T(8,128)(2,1)} %all-gather.5.cloned.1.call-done), channel_id=1, source_target_pairs={{0,16},{16,0},{1,17},{17,1},{2,18},{18,2},{3,19},{19,3},{4,20},{20... | collective-permute-start | bytes 7077896 | tf_op jit(solution)/shard_map/ppermute | solution.py:67
  138.9 1.5 copy-start.9
  138.9 1.5 copy-start.10
  141.1 1.0 copy-start.8
  142.0 3.0 %copy-start.1 = (f32[48,128,64]{1,0,2:T(8,128)S(1)}, f32[48,128,64]{1,0,2:T(8,128)}, u32[]{:S(2)}) copy-start(f32[48,128,64]{1,0,2:T(8,128)} %copy.44) | copy-start | bytes 4718596
  145.4 1.0 copy-start.7
  149.4 0.8 copy-start.11
  178.0 53.6 %all-to-all-start.3 = ((f16[16,4,48,128]{3,1,2,0:T(4,128)(2,1)}), f16[16,4,48,128]{3,1,2,0:T(4,128)(2,1)S(1)}, u32[]{:S(2)}, u32[]{:S(2)}) async-start(f16[16,4,48,128]{3,1,2,0:T(4,128)(2,1)} %copy.47), calls=%async_computation.3 | async-start | bytes 1572864 | tf_op jit(solution)/shard_map/all_to_all | solution.py:109
  185.4 41.9 %copy-start.4 = (bf16[3072,384]{1,0:T(8,128)(2,1)S(1)}, bf16[3072,384]{1,0:T(8,128)(2,1)}, u32[]{:S(2)}) copy-start(bf16[3072,384]{1,0:T(8,128)(2,1)} %all-gather.5.cloned.1.call-done) | copy-start | bytes 7077892
  233.8 2.1 copy-start.14
Sparse Core Ops, SparseCore 0:
  9.6 44.7 all-gather.2
  56.7 54.9 all-gather.4
